TPU v7x, 128 devices: a whole 4x4x4 slice. The times are simulated.
128 devices in a mesh: row: 16 (over z, x), col: 8 (over y, core).
Axes of the slice: x: 4, y: 4, z: 4, core: 2. Of those that a mesh axis runs over, the one named last changes fastest.
Arguments:
- features: bfloat16 [262144, 128], P(('row', 'col')), may hold values from -6 to 6
- tile_values: bfloat16 [65536, 128, 128], P(('row', 'col')), may hold values from 0 to 0.009521484
- tile_row: int32 [65536], P(('row', 'col')), may hold values from 0 to 2047, as said below
- tile_col: int32 [65536], P(('row', 'col')), may hold values from 0 to 2047, as said below
- weight: bfloat16 [128, 256], replicated, may hold values from -0.5 to 0.5
- bias: float32 [256], replicated, may hold values from -3 to 3
Outputs:
- hidden: bfloat16 [262144, 256], P(('row', 'col'))
Inputs may be any that keep to these rules, and one draw needn't show every extreme that they name: Tiles k from 512 * d to 512 * d + 511 belong to device d = 8 * r + c: tile_row[k] // 128 equals r. Coordinates may repeat. For the same tiles, (tile_col[k] // 16) % 8 equals c.
All inputs are finite; a program needn't handle non-finite values.
Results may differ from a plain program's by a relative error of at most 0.0033.
Values may be sent and summed in bfloat16 or wider, within the bound.
A program may use at most 192 MiB of HBM per device.

v0:
```python
import jax
import jax.numpy as jnp
from jax import lax
from jax.sharding import PartitionSpec as P


def local(features, tile_values, tile_row, tile_col, weight, bias):
    row_devices = lax.axis_size("row")
    col_devices = lax.axis_size("col")
    node_count = features.shape[0]
    in_width = features.shape[1]
    tile_size = tile_values.shape[1]
    tile_total = tile_values.shape[0]
    per_slice = node_count // tile_size
    gathered = lax.all_gather(features, "row", axis=0, tiled=True)
    source_tiles = row_devices * per_slice
    gathered = gathered.reshape(source_tiles, tile_size * in_width)
    block_tiles = col_devices * per_slice
    local_row = tile_row % block_tiles
    slice_index = tile_col // per_slice
    local_col = slice_index // col_devices * per_slice + tile_col % per_slice
    pick_table = (local_col[:, None] == jnp.arange(source_tiles, dtype=jnp.int32)[None, :]).astype(
        jnp.bfloat16
    )
    picked = jnp.dot(pick_table, gathered, preferred_element_type=jnp.float32).astype(jnp.bfloat16)
    picked = picked.reshape(tile_total, tile_size, in_width)
    products = jnp.einsum("tij,tjf->tif", tile_values, picked, preferred_element_type=jnp.float32)
    products = products.reshape(tile_total, tile_size * in_width)
    place_table = (local_row[:, None] == jnp.arange(block_tiles, dtype=jnp.int32)[None, :]).astype(
        jnp.float32
    )
    partial_value = lax.dot_general(
        place_table,
        products,
        (((0,), (0,)), ((), ())),
        precision=lax.Precision.HIGHEST,
        preferred_element_type=jnp.float32,
    )
    partial_value = partial_value.reshape(block_tiles * tile_size, in_width)
    summed = lax.psum_scatter(partial_value, "col", scatter_dimension=0, tiled=True)
    aggregate = summed.astype(jnp.bfloat16)
    mixed = jnp.dot(aggregate, weight, preferred_element_type=jnp.float32) + bias
    return jnp.maximum(mixed, 0.0).astype(jnp.bfloat16)


def solution(mesh):
    in_specs = (
        P(("row", "col"), None),
        P(("row", "col"), None, None),
        P(("row", "col")),
        P(("row", "col")),
        P(),
        P(),
    )
    out_specs = P(("row", "col"), None)
    return jax.shard_map(local, mesh=mesh, in_specs=in_specs, out_specs=out_specs, check_vma=False)
```

profile of v0, /device:TPU:0, one launch (start us, length us, event | category | flops | bytes accessed | tf_op | source)
XLA Modules:
  0.0 278.1 jit_solution(9119372184997308738)
XLA Ops:
  6.5 0.0 copy-start
  6.5 0.0 all-gather.2.cloned.1.call-start
  6.5 0.7 all-gather.2.cloned.1.call-update
  7.3 0.0 reduce-scatter.2.cloned.1.call-start
  7.3 0.7 fusion.12
  8.0 0.7 add_select_fusion.3
  8.7 74.2 %all-gather.2.cloned.1.call-done = bf16[32768,128]{1,0:T(8,128)(2,1)} async-done(((bf16[2048,128]{1,0:T(8,128)(2,1)}), bf16[32768,128]{1,0:T(8,128)(2,1)}) %all-gather.2.cloned.1.call-update) | async-done | bytes 8388624 | tf_op jit(solution)/shard_map/all_gather | solution.py:15
  82.9 13.3 %reshape.15 = bf16[256,16384]{1,0:T(8,128)(2,1)} reshape(bf16[32768,128]{1,0:T(8,128)(2,1)} %all-gather.2.cloned.1.call-done) | data formatting | bytes 16777216 | tf_op jit(solution)/shard_map/reshape | solution.py:17
  96.2 11.5 %fusion = bf16[64,8,128,128]{3,1,2,0:T(8,128)(2,1)} fusion(bf16[256,16384]{1,0:T(8,128)(2,1)} %reshape.15, s32[512]{0:T(512)S(1)} %fusion.12), kind=kOutput, calls=%fused_computation.2 | convolution fusion | flops 4303486976 | bytes 25167872 | tf_op jit(solution)/shard_map/dot_general | solution.py:25
  107.7 15.2 %copy.11 = bf16[64,8,128,128]{3,2,1,0:T(8,128)(2,1)} copy(bf16[64,8,128,128]{3,1,2,0:T(8,128)(2,1)} %fusion) | data formatting | bytes 33554432
  122.9 25.2 %convolution_bitcast_fusion = f32[512,128,128]{1,2,0:T(8,128)} fusion(bf16[512,128,128]{2,1,0:T(8,128)(2,1)} %bitcast.12, bf16[512,128,128]{2,1,0:T(8,128)(2,1)} %param.7), kind=kOutput, calls=%fused_computation.1 | convolution fusion | flops 2147483648 | bytes 67108864 | tf_op jit(solution)/shard_map/tij,tjf->tif/dot_general | solution.py:27
  148.0 34.8 %copy.9 = f32[512,128,128]{0,2,1:T(8,128)} copy(f32[512,128,128]{1,2,0:T(8,128)} %convolution_bitcast_fusion) | data formatting | bytes 67108864 | tf_op jit(solution)/shard_map/tij,tjf->tif/dot_general | solution.py:27
  182.8 24.3 %fusion.6 = f32[128,16384]{1,0:T(8,128)} fusion(f32[512,16384]{0,1:T(8,128)} %bitcast.11, s32[512]{0:T(512)S(1)} %add_select_fusion.3), kind=kOutput, calls=%fused_computation.11 | convolution fusion | flops 12885032960 | bytes 41945088 | tf_op jit(solution)/shard_map/dot_general | solution.py:32
  207.2 0.0 copy-start.1
  207.2 9.3 %reshape.18 = f32[16384,128]{1,0:T(8,128)} reshape(f32[128,16384]{1,0:T(8,128)} %fusion.6) | data formatting | bytes 16777216 | tf_op jit(solution)/shard_map/reshape | solution.py:39
  216.4 0.0 reduce-scatter.2.cloned.1.call-update
  216.4 52.2 %reduce-scatter.2.cloned.1.call-done = f32[2048,128]{1,0:T(8,128)} async-done(((f32[16384,128]{1,0:T(8,128)}), f32[2048,128]{1,0:T(8,128)}) %reduce-scatter.2.cloned.1.call-update) | async-done | bytes 1048592 | tf_op jit(solution)/shard_map/reduce_scatter | solution.py:40
  268.6 0.0 copy-done
  268.6 0.0 copy-done.1
  268.6 2.6 fusion.2
Async XLA Ops:
  6.5 262.1 %copy-start = (bf16[128,256]{1,0:T(8,128)(2,1)S(1)}, bf16[128,256]{1,0:T(8,128)(2,1)}, u32[]{:S(2)}) copy-start(bf16[128,256]{1,0:T(8,128)(2,1)} %param.10) | copy-start | bytes 196612
  6.5 76.3 %all-gather.2.cloned.1.call-start = ((), (), s32[]{:S(2)}) async-start(), calls=%async_computation.1 | async-start | bytes 8912896 | tf_op jit(solution)/shard_map/all_gather | solution.py:15
  7.3 261.4 %reduce-scatter.2.cloned.1.call-start = ((), (), s32[]{:S(2)}) async-start(), calls=%async_computation.2 | async-start | bytes 9437184 | tf_op jit(solution)/shard_map/reduce_scatter | solution.py:40
  207.2 61.5 %copy-start.1 = (f32[256]{0:T(256)S(1)}, f32[256]{0:T(256)}, u32[]{:S(2)}) copy-start(f32[256]{0:T(256)} %param.11) | copy-start | bytes 3076
Sparse Core Ops, SparseCore 0:
  9.5 73.3 all-gather.1
  216.6 52.0 reduce-scatter.1
where the time goes:
time: 280 us; the launch traced here: 278 us
  waiting for transfers between devices  127 us (45%)
  local copies, waits for them, and re-layouts  72.6 us (26%)
  matrix products  63.6 us (23%)
  between operations  13.4 us (5%)
    all_gather x1, waiting for transfers between devices, local(): gathered = lax.all_gather(features, 'row', axis=0, tiled=True)  74.2 us
    reduce_scatter x1, waiting for transfers between devices, local(): lax.psum_scatter(partial_value, 'col', scatter_dimension=0, tiled=True)  52.2 us
    dot_general x1, local copies, waits for them, and re-layouts, local(): jnp.einsum('tij,tjf->tif', tile_values, picked, preferred_element_type=jn...  34.8 us
    dot_general x1, matrix products, local(): jnp.einsum('tij,tjf->tif', tile_values, picked, preferred_element_type=jn...  25.2 us
    dot_general x1, matrix products, local(): lax.dot_general(place_table, products, (((0,), (0,)), ((), ())), precisio...  24.3 us
    unnamed x5, local copies, waits for them, and re-layouts  15.2 us
    reshape x1, local copies, waits for them, and re-layouts, local(): gathered = gathered.reshape(source_tiles, tile_size * in_width)  13.3 us
    dot_general x1, matrix products, local(): jnp.dot(pick_table, gathered, preferred_element_type=jnp.float32)  11.5 us
  transfers between devices with their start and end apart: 2, of which 2 were waited for; matrix products, arithmetic and copies ran while one was open for 1% of the time, Pallas kernels for 0%

commit v1 on v0

v1 whole, which is shorter than its diff:
```python
import jax
import jax.numpy as jnp
from jax import lax
from jax.experimental import pallas as pl
from jax.experimental.pallas import tpu as pltpu
from jax.sharding import PartitionSpec as P

MESH = pl.DeviceIdType.MESH
NN = (((1,), (0,)), ((), ()))

T = 128
TILES = 512
PAIRS = 320
ROWS = 128
OWN = 16
CHUNKS = (48, 48, 32)
SENT_AS = (jnp.float32, jnp.bfloat16, jnp.bfloat16)
STAGE = 32
STAGES = TILES // STAGE
SLOTS = 4
UNROLL = 32
MSG = 20
F32 = jnp.float32
BF16 = jnp.bfloat16
I32 = jnp.int32


def column(line):
    return jnp.broadcast_to(line, (T, T)).T


def plan_tiles(trow_ref, tcol_ref, plan_v, last_v):
    row = trow_ref[...] & (ROWS - 1)
    tcol = tcol_ref[...]
    at_z, at_x = (tcol >> 9) & 3, (tcol >> 7) & 3
    col = ((at_z & 1) << 7) | ((at_z >> 1) << 6) | ((at_x & 1) << 5) | ((at_x >> 1) << 4) | (tcol & 15)
    k = lax.broadcasted_iota(I32, (1, TILES), 1)
    key = row * TILES + k
    packed = k + (row << 10) + (col << 17) + 1
    lane = lax.broadcasted_iota(I32, (T, T), 1)
    sub = lax.broadcasted_iota(I32, (T, T), 0)
    blocks = [slice(b * T, (b + 1) * T) for b in range(TILES // T)]
    row_s = [column(row[:, b]) for b in blocks]
    key_s = [column(key[:, b]) for b in blocks]
    count = jnp.zeros((1, T), I32)
    for b in range(len(blocks)):
        count += jnp.sum(jnp.where(row_s[b] == lane, 1, 0), axis=0, keepdims=True)
    pairs = (count + 1) >> 1
    odd = 2 * pairs - count
    through = jnp.sum(jnp.where(sub <= lane, column(pairs), 0), axis=0, keepdims=True)
    last_v[...] = jnp.where(count > 0, through - 1, -1)
    total = jnp.zeros((1, 2 * PAIRS), I32)
    place = lax.broadcasted_iota(I32, (T, 2 * PAIRS), 1)
    for b in range(len(blocks)):
        at = jnp.sum(jnp.where(lane < row_s[b], odd, 0), axis=1, keepdims=True)
        for other in blocks:
            at += jnp.sum(jnp.where(key[:, other] < key_s[b], 1, 0), axis=1, keepdims=True)
        packed_s = jnp.concatenate([column(packed[:, blocks[b]])] * (2 * PAIRS // T), axis=1)
        total += jnp.sum(jnp.where(place == at, packed_s, 0), axis=0, keepdims=True)
    plan_v[...] = jnp.where(total == 0, TILES, total - 1)


def kernel(feat_ref, tiles_hbm, trow_ref, tcol_ref, out_ref, *scratch):
    q_count = len(CHUNKS)
    scratch = list(scratch)
    take = lambda n: [scratch.pop(0) for _ in range(n)]
    xs = take(q_count)
    csend, crecv, own, ysend, yrecv = (take(q_count) for _ in range(5))
    at, stage, slots, agg, plan_v, last_v, plan, last = take(8)
    gsend, grecv, csem_s, csem_r, ysem_s, ysem_r, stage_sem, plan_sem = take(8)

    row, col = lax.axis_index("row"), lax.axis_index("col")
    z, x = row // 4, row % 4
    y, core = col // 2, col % 2

    def row_at(dz, dx):
        return ((z + dz + 4) % 4) * 4 + (x + dx + 4) % 4

    def col_at(dy, c):
        return ((y + dy + 4) % 4) * 2 + c

    def spot(i):
        return (i % 2) * 2 + i // 2

    plane = {d: (row_at(*d), col) for d in ((1, 0), (-1, 0), (0, 1), (0, -1))}
    sibling = (row, y * 2 + 1 - core)
    up, down = (row, col_at(1, core)), (row, col_at(-1, core))

    def load(s):
        return pltpu.make_async_copy(
            tiles_hbm.at[pl.ds(s * STAGE, STAGE)], stage.at[s % SLOTS], stage_sem.at[s % SLOTS]
        )

    for s in range(SLOTS):
        load(s).start()

    barrier = pltpu.get_barrier_semaphore()
    partners = list(plane.values()) + [sibling, up, down]
    for partner in partners:
        pl.semaphore_signal(barrier, inc=1, device_id=partner, device_id_type=MESH)

    for t in range(OWN):
        block = feat_ref[t * T:(t + 1) * T, :].T
        start = 0
        for q, width in enumerate(CHUNKS):
            xs[q][spot(z), spot(x), t] = block[start:start + width]
            start += width

    pl.semaphore_wait(barrier, len(partners))

    def piece_of(q, piece, dz, dx):
        kind, t0, n = piece
        zi, xi = spot((z + dz + 4) % 4), spot((x + dx + 4) % 4)
        if kind == "shard":
            return xs[q].at[zi, xi, pl.ds(t0, n)]
        axis, near = kind
        start = 2 * ((((z + dz + 4) if axis == 0 else (x + dx + 4)) + near) % 2)
        if axis == 0:
            return xs[q].at[pl.ds(start, 2), xi, pl.ds(t0, n)]
        return xs[q].at[zi, pl.ds(start, 2), pl.ds(t0, n)]

    def message(q, m, direction, dz, dx, piece):
        part = piece_of(q, piece, dz, dx)
        return pltpu.make_async_remote_copy(
            src_ref=part, dst_ref=part, send_sem=gsend.at[q, m], recv_sem=grecv.at[q, m],
            device_id=plane[direction], device_id_type=MESH,
        )

    def gather(q):
        table = {}
        for half in range(2):
            first = (lambda s: (s, 0)) if half == 0 else (lambda s: (0, s))
            second = (lambda s: (0, s)) if half == 0 else (lambda s: (s, 0))
            t0, m0 = 8 * half, 10 * half
            near, far = ((half, 1), t0, 8), ((half, 0), t0, 8)
            table[m0 + 0] = (first(1), (0, 0), ("shard", t0, 8))
            table[m0 + 1] = (first(-1), (0, 0), ("shard", t0, 8))
            table[m0 + 2] = (first(1), first(-1), ("shard", t0, 4))
            table[m0 + 3] = (first(-1), first(1), ("shard", t0 + 4, 4))
            table[m0 + 4] = (second(1), (0, 0), near)
            table[m0 + 5] = (second(-1), (0, 0), near)
            table[m0 + 6] = (second(1), (0, 0), far)
            table[m0 + 7] = (second(-1), (0, 0), far)
            table[m0 + 8] = (second(1), second(-1), near)
            table[m0 + 9] = (second(-1), second(1), far)

        def send(*ms):
            for m in ms:
                direction, (dz, dx), piece = table[m]
                message(q, m, direction, dz, dx, piece).start()

        def arrive(*ms):
            for m in ms:
                direction, (dz, dx), piece = table[m]
                message(q, m, direction, dz - direction[0], dx - direction[1], piece).wait_recv()

        def sent():
            for m in table:
                direction, (dz, dx), piece = table[m]
                message(q, m, direction, dz, dx, piece).wait_send()

        def both(waits, sends):
            def run():
                for h in (0, 10):
                    arrive(*[h + m for m in waits])
                    send(*[h + m for m in sends])
            return run

        return dict(
            own=lambda: send(0, 10, 1, 11),
            hop=lambda: (both([0], [2])(), both([1], [3])()),
            near=both([], [4, 5]),
            far=both([2, 3], [6, 7]),
            near2=both([4], [8]),
            far2=both([7], [9]),
            end=both([5, 6, 8, 9], []),
            sent=sent,
        )

    gathers = [gather(q) for q in range(q_count)]

    def turn(s):
        def run():
            load(s).wait()

            def body(g, carry):
                for u in range(8):
                    i = g * 8 + u
                    at[s * STAGE + i] = stage[s % SLOTS, i].T
                return carry

            lax.fori_loop(0, STAGE // 8, body, 0)
            if s + SLOTS < STAGES:
                load(s + SLOTS).start()
        return run

    def prepare():
        plan_tiles(trow_ref, tcol_ref, plan_v, last_v)
        one = pltpu.make_async_copy(plan_v, plan, plan_sem.at[0])
        two = pltpu.make_async_copy(last_v, last, plan_sem.at[1])
        one.start()
        two.start()
        at[TILES] = jnp.zeros((T, T), BF16)
        one.wait()
        two.wait()

    def products(q, p0, n):
        width = CHUNKS[q]

        def run():
            def body(g, total):
                for u in range(UNROLL):
                    p = p0 + g * UNROLL + u
                    one, two = plan[0, 2 * p], plan[0, 2 * p + 1]
                    before = plan[0, jnp.maximum(2 * p - 2, 0)]
                    left = jnp.concatenate([pick(q, one), pick(q, two)], axis=1)
                    right = jnp.concatenate([turned(one), turned(two)], axis=0)
                    product = lax.dot_general(left, right, NN, preferred_element_type=F32)
                    same = ((one >> 10) & 127) == ((before >> 10) & 127)
                    total = jnp.where(same, total, 0.0) + product
                    slots[p, 0:width] = total
                return total

            first = jnp.zeros((width, T), F32) if p0 == 0 else slots[p0 - 1, 0:width]
            lax.fori_loop(0, n // UNROLL, body, first)
        return run

    def pick(q, entry):
        return xs[q][(entry >> 23) & 3, (entry >> 21) & 3, (entry >> 17) & 15]

    def turned(entry):
        return at[jnp.minimum(entry & 1023, TILES)]

    ORDER = (2, -1, 1, 0)

    def core_copy(q, o):
        return pltpu.make_async_remote_copy(
            src_ref=csend[q].at[o], dst_ref=crecv[q].at[o], send_sem=csem_s.at[q, o], recv_sem=csem_r.at[q, o],
            device_id=sibling, device_id_type=MESH,
        )

    def extract(q):
        width = CHUNKS[q]

        def part(o, which, target):
            base = (((y + ORDER[o] + 4) % 4) * 2 + which) * OWN

            def body(g, carry):
                for u in range(8):
                    t = g * 8 + u
                    p = last[0, base + t]
                    value = slots[jnp.clip(p, 0, PAIRS - 1), 0:width]
                    target[o, t] = jnp.where(p >= 0, value, 0.0)
                return carry

            lax.fori_loop(0, OWN // 8, body, 0)

        def run():
            for o in range(4):
                part(o, 1 - core, csend[q])
                core_copy(q, o).start()
            for o in range(4):
                part(o, core, own[q])
        return run

    Y_TARGET = (down, up, down, up, down, up)

    def y_copy(q, n):
        return pltpu.make_async_remote_copy(
            src_ref=ysend[q].at[n], dst_ref=yrecv[q].at[n], send_sem=ysem_s.at[q, n], recv_sem=ysem_r.at[q, n],
            device_id=Y_TARGET[n], device_id_type=MESH,
        )

    def joined(q, o, t0):
        return own[q][o, t0:t0 + 8] + crecv[q][o, t0:t0 + 8]

    def reduce_first(q):
        def run():
            core_copy(q, 0).wait_recv()
            for n in range(2):
                ysend[q][n] = joined(q, 0, 8 * n).astype(SENT_AS[q])
                y_copy(q, n).start()
            core_copy(q, 1).wait_recv()
            ysend[q][2] = joined(q, 1, 8).astype(SENT_AS[q])
            y_copy(q, 2).start()
            core_copy(q, 2).wait_recv()
            ysend[q][3] = joined(q, 2, 0).astype(SENT_AS[q])
            y_copy(q, 3).start()
        return run

    def reduce_second(q):
        def run():
            for n, o, t0 in ((4, 1, 0), (5, 2, 8)):
                y_copy(q, n - 4).wait_recv()
                ysend[q][n] = (joined(q, o, t0) + yrecv[q][n - 4].astype(F32)).astype(SENT_AS[q])
                y_copy(q, n).start()
        return run

    def reduce_last(q):
        start = sum(CHUNKS[:q])

        def run():
            core_copy(q, 3).wait_recv()
            for half, direct, summed in ((0, 3, 4), (1, 2, 5)):
                y_copy(q, direct).wait_recv()
                y_copy(q, summed).wait_recv()
                t0 = 8 * half
                value = joined(q, 3, t0) + yrecv[q][direct].astype(F32) + yrecv[q][summed].astype(F32)
                agg[t0:t0 + 8, start:start + CHUNKS[q]] = value.astype(BF16)
        return run

    step = 2 * UNROLL
    steps = {"plan": prepare}
    for s in range(STAGES):
        steps["turn%d" % s] = turn(s)
    for q in range(q_count):
        for name, run in gathers[q].items():
            steps["%d%s" % (q, name)] = run
        for b in range(PAIRS // step):
            steps["%db%d" % (q, b)] = products(q, b * step, step)
        for name, make in (("cut", extract), ("y1", reduce_first), ("y2", reduce_second), ("y3", reduce_last)):
            steps["%d%s" % (q, name)] = make(q)

    def turns(a, b):
        return ["turn%d" % s for s in range(a, b)]

    order = ["0own", "1own", "plan", "0hop", "0near", *turns(0, 4), "0far", *turns(4, 8), "1hop", *turns(8, 10)]
    order += ["0near2", "2own", *turns(10, 13), "0far2", "1near", "1far", *turns(13, 16), "0end"]
    for q in range(1, q_count):
        p, r, n, m = q - 1, q - 2, q + 1, q + 2
        order += [f"{n}hop", f"{p}b0", f"{p}b1", f"{p}b2", f"{q}near2", f"{m}own", f"{p}b3", f"{p}b4", f"{p}cut"]
        order += [f"{q}far2", f"{n}near", f"{n}far", f"{p}y1", f"{r}y3"]
        order += [f"{q}end"] if q == q_count - 1 else [f"{p}y2", f"{q}end"]
    q, p = q_count - 1, q_count - 2
    order += [f"{q}b0", f"{p}y2", f"{q}b1", f"{q}b2", f"{q}b3", f"{q}b4", f"{q}cut"]
    order += [f"{p}y3", f"{q}y1", f"{q}y2", f"{q}y3"]
    for name in order:
        if name in steps:
            steps[name]()

    for t in range(OWN):
        out_ref[t * T:(t + 1) * T, :] = agg[t].T

    for q in range(q_count):
        gathers[q]["sent"]()
        for o in range(4):
            core_copy(q, o).wait_send()
        for n in range(6):
            y_copy(q, n).wait_send()


def local(features, tile_values, tile_row, tile_col, weight, bias):
    vmem = pl.BlockSpec(memory_space=pltpu.VMEM)
    q_count = len(CHUNKS)
    widest = max(CHUNKS)
    dma = pltpu.SemaphoreType.DMA
    scratch = [pltpu.VMEM((4, 4, OWN, f, T), BF16) for f in CHUNKS]
    for kind in range(3):
        scratch += [pltpu.VMEM((4, OWN, f, T), F32) for f in CHUNKS]
    for kind in range(2):
        scratch += [pltpu.VMEM((6, 8, f, T), kept) for f, kept in zip(CHUNKS, SENT_AS)]
    scratch += [
        pltpu.VMEM((TILES + 1, T, T), BF16),
        pltpu.VMEM((SLOTS, STAGE, T, T), BF16),
        pltpu.VMEM((PAIRS, widest, T), F32),
        pltpu.VMEM((OWN, T, T), BF16),
        pltpu.VMEM((1, 2 * PAIRS), I32),
        pltpu.VMEM((1, T), I32),
        pltpu.SMEM((1, 2 * PAIRS), I32),
        pltpu.SMEM((1, T), I32),
        dma((q_count, MSG)),
        dma((q_count, MSG)),
        dma((q_count, 4)),
        dma((q_count, 4)),
        dma((q_count, 6)),
        dma((q_count, 6)),
        dma((SLOTS,)),
        dma((2,)),
    ]
    aggregate = pl.pallas_call(
        kernel,
        out_shape=jax.ShapeDtypeStruct((OWN * T, T), BF16),
        in_specs=[vmem, pl.BlockSpec(memory_space=pl.ANY), vmem, vmem],
        out_specs=vmem,
        scratch_shapes=scratch,
        compiler_params=pltpu.CompilerParams(
            collective_id=0, has_side_effects=True, vmem_limit_bytes=60 * 2**20
        ),
        cost_estimate=pl.CostEstimate(flops=2 * 10**9, bytes_accessed=19 * 10**6, transcendentals=0),
        name="graph_layer",
    )(features, tile_values, tile_row.reshape(1, TILES), tile_col.reshape(1, TILES))
    mixed = jnp.dot(aggregate, weight, preferred_element_type=F32) + bias
    return jnp.maximum(mixed, 0.0).astype(BF16)


def solution(mesh):
    in_specs = (
        P(("row", "col"), None),
        P(("row", "col"), None, None),
        P(("row", "col")),
        P(("row", "col")),
        P(),
        P(),
    )
    return jax.shard_map(local, mesh=mesh, in_specs=in_specs, out_specs=P(("row", "col"), None), check_vma=False)
```

time: 280 us -> 80.8 us (0.29)
  waiting for transfers between devices: 127 us -> 0 us
  Pallas kernels: 0 us -> 78.2 us
  local copies, waits for them, and re-layouts: 72.6 us -> 0.01 us
  matrix products: 63.6 us -> 2.43 us
  between operations: 13.4 us -> 0.03 us
    pallas_call x0 -> x1, Pallas kernels: none -> 78.2 us  [local(): pl.pallas_call(kernel, out_shape=jax.ShapeDtypeStruct((OWN * T, T), BF16)...]
    all_gather x1 -> x0, waiting for transfers between devices: 74.2 us -> none  [local(): gathered = lax.all_gather(features, 'row', axis=0, tiled=True)]
    dot_general x4 -> x1, matrix products: 63.6 us -> 2.43 us  [local(): mixed = jnp.dot(aggregate, weight, preferred_element_type=F32) + bias]
    reduce_scatter x1 -> x0, waiting for transfers between devices: 52.2 us -> none  [local(): lax.psum_scatter(partial_value, 'col', scatter_dimension=0, tiled=True)]
    dot_general x1 -> x0, local copies, waits for them, and re-layouts: 34.8 us -> none  [local(): jnp.einsum('tij,tjf->tif', tile_values, picked, preferred_element_type=jn...]
    reshape x2 -> x0, local copies, waits for them, and re-layouts: 22.6 us -> none  [the longest x1 13.3 us: local(): gathered = gathered.reshape(source_tiles, tile_size * in_width)]
    unnamed x5 -> x4, local copies, waits for them, and re-layouts: 15.2 us -> 0.01 us
  transfers between devices with their start and end apart: 2 -> 0, of which waited for: 2 -> 0; matrix products, arithmetic and copies ran while one was open for 1% -> 0% of each run, Pallas kernels for 0% -> 0%
where the time goes in v1:
time: 80.8 us; the launch traced here: 80.6 us
  Pallas kernels  78.2 us (97%)
  matrix products  2.43 us (3%)
    pallas_call x1, Pallas kernels, local(): pl.pallas_call(kernel, out_shape=jax.ShapeDtypeStruct((OWN * T, T), BF16)...  78.2 us
    dot_general x1, matrix products, local(): mixed = jnp.dot(aggregate, weight, preferred_element_type=F32) + bias  2.43 us

profile of v1, /device:TPU:0, one launch (start us, length us, event | category | flops | bytes accessed | tf_op | source)
XLA Modules:
  0.0 80.6 jit_solution(300061293699323649)
XLA Ops:
  0.0 0.0 copy-start
  0.0 0.0 copy-start.1
  0.0 78.2 %graph_layer.1 = bf16[2048,128]{1,0:T(8,128)(2,1)} custom-call(bf16[2048,128]{1,0:T(8,128)(2,1)} %feat_ref.1, bf16[512,128,128]{2,1,0:T(8,128)(2,1)} %tiles_hbm.1, s32[1,512]{1,0:T(1,128)} %bitcast.4, s32[1,512]{1,0:T(1,128)} %bitcast.5), custom_call_target="tpu_custom_call" | custom-call | flops 2000000000 | bytes 19000000 | tf_op jit(solution)/shard_map/graph_layer/pallas_call | solution.py:380
  78.2 0.0 copy-done
  78.2 0.0 copy-done.1
  78.2 2.4 %fusion.1 = bf16[2048,256]{1,0:T(8,128)(2,1)} fusion(bf16[2048,128]{1,0:T(8,128)(2,1)} %graph_layer.1, bf16[128,256]{1,0:T(8,128)(2,1)S(1)} %copy-done, f32[256]{0:T(256)S(1)} %copy-done.1), kind=kOutput, calls=%fused_computation.2 | convolution fusion | flops 135790592 | bytes 1639424 | tf_op jit(solution)/shard_map/dot_general | solution.py:392
Async XLA Ops:
  0.0 78.2 %copy-start = (bf16[128,256]{1,0:T(8,128)(2,1)S(1)}, bf16[128,256]{1,0:T(8,128)(2,1)}, u32[]{:S(2)}) copy-start(bf16[128,256]{1,0:T(8,128)(2,1)} %param.10) | copy-start | bytes 196612
  0.0 78.2 %copy-start.1 = (f32[256]{0:T(256)S(1)}, f32[256]{0:T(256)}, u32[]{:S(2)}) copy-start(f32[256]{0:T(256)} %param.11) | copy-start | bytes 3076

commit v2 on v1

--- a/solution.py
+++ b/solution.py
@@ -13,13 +13,24 @@
 PAIRS = 320
 ROWS = 128
 OWN = 16
-CHUNKS = (48, 48, 32)
-SENT_AS = (jnp.float32, jnp.bfloat16, jnp.bfloat16)
+CHUNKS = (32, 32, 32, 32)
+SENT_AS = (jnp.float32, jnp.float32, jnp.bfloat16, jnp.bfloat16)
+PAIRED_AS = (jnp.float32, jnp.float32, jnp.float32, jnp.bfloat16)
+SCHEDULE = (
+    "0own", "1own", "2own", "load", "plan", "turn0", "turn1", "0hop", "0near", "turn2", "turn3", "turn4", "turn5",
+    "turn6", "turn7", "turn8", "turn9", "0far", "1hop", "turn10", "turn11", "turn12", "turn13", "turn14", "turn15",
+    "0near2", "0far2", "1wide", "2hop", "0end", "0b0", "1near2", "3own", "0b1", "0b2", "1far2", "0b3", "0b4", "0cut",
+    "2wide", "0y1", "3hop", "1end", "1b0", "2near2", "0y2", "1b1", "1b2", "2far2", "1b3", "1b4", "1cut", "3wide",
+    "0y3", "1y1", "2end", "2b0", "2b1", "2b2", "3near2", "3far2", "1y2", "2b3", "2b4", "2cut", "2y1", "3end", "3b0",
+    "2y2", "3cut", "1y3", "3y1", "2y3", "3y2", "3y3",
+)
 STAGE = 32
 STAGES = TILES // STAGE
 SLOTS = 4
 UNROLL = 32
+BLOCKS = 5
 MSG = 20
+OUT_PARTS = 8
 F32 = jnp.float32
 BF16 = jnp.bfloat16
 I32 = jnp.int32
@@ -60,14 +71,14 @@
     plan_v[...] = jnp.where(total == 0, TILES, total - 1)
 
 
-def kernel(feat_ref, tiles_hbm, trow_ref, tcol_ref, out_ref, *scratch):
+def kernel(feat_hbm, tiles_hbm, trow_hbm, tcol_hbm, out_ref, *scratch):
     q_count = len(CHUNKS)
     scratch = list(scratch)
     take = lambda n: [scratch.pop(0) for _ in range(n)]
     xs = take(q_count)
     csend, crecv, own, ysend, yrecv = (take(q_count) for _ in range(5))
-    at, stage, slots, agg, plan_v, last_v, plan, last = take(8)
-    gsend, grecv, csem_s, csem_r, ysem_s, ysem_r, stage_sem, plan_sem = take(8)
+    at, stage, slots, agg, plan_v, last_v, plan, last, feat_ref, trow_ref, tcol_ref = take(11)
+    gsend, grecv, csem_s, csem_r, ysem_s, ysem_r, stage_sem, plan_sem, feat_sem = take(9)
 
     row, col = lax.axis_index("row"), lax.axis_index("col")
     z, x = row // 4, row % 4
@@ -91,15 +102,26 @@
             tiles_hbm.at[pl.ds(s * STAGE, STAGE)], stage.at[s % SLOTS], stage_sem.at[s % SLOTS]
         )
 
-    for s in range(SLOTS):
-        load(s).start()
-
     barrier = pltpu.get_barrier_semaphore()
     partners = list(plane.values()) + [sibling, up, down]
     for partner in partners:
         pl.semaphore_signal(barrier, inc=1, device_id=partner, device_id_type=MESH)
 
+    def half_features(h):
+        rows = pl.ds(h * OWN * T // 2, OWN * T // 2)
+        return pltpu.make_async_copy(feat_hbm.at[rows], feat_ref.at[rows], feat_sem.at[h])
+
+    coordinates = [
+        pltpu.make_async_copy(trow_hbm, trow_ref, feat_sem.at[2]),
+        pltpu.make_async_copy(tcol_hbm, tcol_ref, feat_sem.at[3]),
+    ]
+    for h in range(2):
+        half_features(h).start()
+    for copy in coordinates:
+        copy.start()
     for t in range(OWN):
+        if t % (OWN // 2) == 0:
+            half_features(t // (OWN // 2)).wait()
         block = feat_ref[t * T:(t + 1) * T, :].T
         start = 0
         for q, width in enumerate(CHUNKS):
@@ -171,6 +193,7 @@
             hop=lambda: (both([0], [2])(), both([1], [3])()),
             near=both([], [4, 5]),
             far=both([2, 3], [6, 7]),
+            wide=both([2, 3], [4, 7, 6, 5]),
             near2=both([4], [8]),
             far2=both([7], [9]),
             end=both([5, 6, 8, 9], []),
@@ -195,6 +218,8 @@
         return run
 
     def prepare():
+        for copy in coordinates:
+            copy.wait()
         plan_tiles(trow_ref, tcol_ref, plan_v, last_v)
         one = pltpu.make_async_copy(plan_v, plan, plan_sem.at[0])
         two = pltpu.make_async_copy(last_v, last, plan_sem.at[1])
@@ -204,13 +229,13 @@
         one.wait()
         two.wait()
 
-    def products(q, p0, n):
+    def products(q, p0, n, unroll=UNROLL):
         width = CHUNKS[q]
 
         def run():
             def body(g, total):
-                for u in range(UNROLL):
-                    p = p0 + g * UNROLL + u
+                for u in range(unroll):
+                    p = p0 + g * unroll + u
                     one, two = plan[0, 2 * p], plan[0, 2 * p + 1]
                     before = plan[0, jnp.maximum(2 * p - 2, 0)]
                     left = jnp.concatenate([pick(q, one), pick(q, two)], axis=1)
@@ -222,7 +247,7 @@
                 return total
 
             first = jnp.zeros((width, T), F32) if p0 == 0 else slots[p0 - 1, 0:width]
-            lax.fori_loop(0, n // UNROLL, body, first)
+            lax.fori_loop(0, n // unroll, body, first)
         return run
 
     def pick(q, entry):
@@ -250,7 +275,7 @@
                     t = g * 8 + u
                     p = last[0, base + t]
                     value = slots[jnp.clip(p, 0, PAIRS - 1), 0:width]
-                    target[o, t] = jnp.where(p >= 0, value, 0.0)
+                    target[o, t] = jnp.where(p >= 0, value, 0.0).astype(target.dtype)
                 return carry
 
             lax.fori_loop(0, OWN // 8, body, 0)
@@ -272,7 +297,7 @@
         )
 
     def joined(q, o, t0):
-        return own[q][o, t0:t0 + 8] + crecv[q][o, t0:t0 + 8]
+        return own[q][o, t0:t0 + 8] + crecv[q][o, t0:t0 + 8].astype(F32)
 
     def reduce_first(q):
         def run():
@@ -309,34 +334,25 @@
                 agg[t0:t0 + 8, start:start + CHUNKS[q]] = value.astype(BF16)
         return run
 
-    step = 2 * UNROLL
-    steps = {"plan": prepare}
+    def begin():
+        for s in range(SLOTS):
+            load(s).start()
+
+    steps = {"load": begin, "plan": prepare}
     for s in range(STAGES):
         steps["turn%d" % s] = turn(s)
     for q in range(q_count):
         for name, run in gathers[q].items():
             steps["%d%s" % (q, name)] = run
-        for b in range(PAIRS // step):
-            steps["%db%d" % (q, b)] = products(q, b * step, step)
+        blocks = BLOCKS if q < q_count - 1 else 1
+        step = PAIRS // blocks
+        for b in range(blocks):
+            steps["%db%d" % (q, b)] = products(q, b * step, step, UNROLL if blocks > 1 else 2 * UNROLL)
         for name, make in (("cut", extract), ("y1", reduce_first), ("y2", reduce_second), ("y3", reduce_last)):
             steps["%d%s" % (q, name)] = make(q)
 
-    def turns(a, b):
-        return ["turn%d" % s for s in range(a, b)]
-
-    order = ["0own", "1own", "plan", "0hop", "0near", *turns(0, 4), "0far", *turns(4, 8), "1hop", *turns(8, 10)]
-    order += ["0near2", "2own", *turns(10, 13), "0far2", "1near", "1far", *turns(13, 16), "0end"]
-    for q in range(1, q_count):
-        p, r, n, m = q - 1, q - 2, q + 1, q + 2
-        order += [f"{n}hop", f"{p}b0", f"{p}b1", f"{p}b2", f"{q}near2", f"{m}own", f"{p}b3", f"{p}b4", f"{p}cut"]
-        order += [f"{q}far2", f"{n}near", f"{n}far", f"{p}y1", f"{r}y3"]
-        order += [f"{q}end"] if q == q_count - 1 else [f"{p}y2", f"{q}end"]
-    q, p = q_count - 1, q_count - 2
-    order += [f"{q}b0", f"{p}y2", f"{q}b1", f"{q}b2", f"{q}b3", f"{q}b4", f"{q}cut"]
-    order += [f"{p}y3", f"{q}y1", f"{q}y2", f"{q}y3"]
-    for name in order:
-        if name in steps:
-            steps[name]()
+    for name in SCHEDULE:
+        steps[name]()
 
     for t in range(OWN):
         out_ref[t * T:(t + 1) * T, :] = agg[t].T
@@ -349,14 +365,28 @@
             y_copy(q, n).wait_send()
 
 
+def mix(agg_ref, w_ref, bias_ref, out_hbm, out_v, sem):
+    rows = OWN * T // OUT_PARTS
+    copies = []
+    for i in range(OUT_PARTS):
+        part = pl.ds(i * rows, rows)
+        mixed = lax.dot_general(agg_ref[part, :], w_ref[...], NN, preferred_element_type=F32) + bias_ref[...]
+        out_v[part, :] = jnp.maximum(mixed, 0.0).astype(BF16)
+        copies.append(pltpu.make_async_copy(out_v.at[part], out_hbm.at[part], sem.at[i]))
+        copies[-1].start()
+    for copy in copies:
+        copy.wait()
+
+
 def local(features, tile_values, tile_row, tile_col, weight, bias):
     vmem = pl.BlockSpec(memory_space=pltpu.VMEM)
     q_count = len(CHUNKS)
     widest = max(CHUNKS)
     dma = pltpu.SemaphoreType.DMA
     scratch = [pltpu.VMEM((4, 4, OWN, f, T), BF16) for f in CHUNKS]
-    for kind in range(3):
-        scratch += [pltpu.VMEM((4, OWN, f, T), F32) for f in CHUNKS]
+    for kind in range(2):
+        scratch += [pltpu.VMEM((4, OWN, f, T), kept) for f, kept in zip(CHUNKS, PAIRED_AS)]
+    scratch += [pltpu.VMEM((4, OWN, f, T), F32) for f in CHUNKS]
     for kind in range(2):
         scratch += [pltpu.VMEM((6, 8, f, T), kept) for f, kept in zip(CHUNKS, SENT_AS)]
     scratch += [
@@ -368,6 +398,9 @@
         pltpu.VMEM((1, T), I32),
         pltpu.SMEM((1, 2 * PAIRS), I32),
         pltpu.SMEM((1, T), I32),
+        pltpu.VMEM((OWN * T, T), BF16),
+        pltpu.VMEM((1, TILES), I32),
+        pltpu.VMEM((1, TILES), I32),
         dma((q_count, MSG)),
         dma((q_count, MSG)),
         dma((q_count, 4)),
@@ -376,11 +409,12 @@
         dma((q_count, 6)),
         dma((SLOTS,)),
         dma((2,)),
+        dma((4,)),
     ]
     aggregate = pl.pallas_call(
         kernel,
-        out_shape=jax.ShapeDtypeStruct((OWN * T, T), BF16),
-        in_specs=[vmem, pl.BlockSpec(memory_space=pl.ANY), vmem, vmem],
+        out_shape=pltpu.VMEM((OWN * T, T), BF16),
+        in_specs=[pl.BlockSpec(memory_space=pl.ANY)] * 4,
         out_specs=vmem,
         scratch_shapes=scratch,
         compiler_params=pltpu.CompilerParams(
@@ -389,8 +423,16 @@
         cost_estimate=pl.CostEstimate(flops=2 * 10**9, bytes_accessed=19 * 10**6, transcendentals=0),
         name="graph_layer",
     )(features, tile_values, tile_row.reshape(1, TILES), tile_col.reshape(1, TILES))
-    mixed = jnp.dot(aggregate, weight, preferred_element_type=F32) + bias
-    return jnp.maximum(mixed, 0.0).astype(BF16)
+    return pl.pallas_call(
+        mix,
+        out_shape=jax.ShapeDtypeStruct((OWN * T, 2 * T), BF16),
+        in_specs=[vmem] * 3,
+        out_specs=pl.BlockSpec(memory_space=pl.ANY),
+        scratch_shapes=[pltpu.VMEM((OWN * T, 2 * T), BF16), dma((OUT_PARTS,))],
+        compiler_params=pltpu.CompilerParams(vmem_limit_bytes=8 * 2**20),
+        cost_estimate=pl.CostEstimate(flops=2 * 10**8, bytes_accessed=2 * 10**6, transcendentals=0),
+        name="mix",
+    )(aggregate, weight, bias.reshape(1, -1))
 
 
 def solution(mesh):

time: 80.8 us -> 74.2 us (0.918)
  Pallas kernels: 78.2 us -> 73.9 us
  matrix products: 2.43 us -> 0 us
    pallas_call x1 -> x2, Pallas kernels: 78.2 us -> 73.9 us  [the longest x1 72.6 us: local(): pl.pallas_call(kernel, out_shape=pltpu.VMEM((OWN * T, T), BF16), in_specs...]
    dot_general x1 -> x0, matrix products: 2.43 us -> none  [local(): mixed = jnp.dot(aggregate, weight, preferred_element_type=F32) + bias]
where the time goes in v2:
time: 74.2 us; the launch traced here: 74.1 us
  Pallas kernels  73.9 us (100%)
    pallas_call x1, Pallas kernels, local(): pl.pallas_call(kernel, out_shape=pltpu.VMEM((OWN * T, T), BF16), in_specs...  72.6 us

profile of v2, /device:TPU:0, one launch (start us, length us, event | category | flops | bytes accessed | tf_op | source)
XLA Modules:
  0.0 74.1 jit_solution(10217410755093148375)
XLA Ops:
  0.0 0.0 copy-start.1
  0.0 0.0 copy-start
  0.0 72.6 %graph_layer.1.agg_ref = bf16[2048,128]{1,0:T(8,128)(2,1)S(1)} custom-call(bf16[2048,128]{1,0:T(8,128)(2,1)} %feat_hbm.1, bf16[512,128,128]{2,1,0:T(8,128)(2,1)} %tiles_hbm.1, s32[1,512]{1,0:T(1,128)} %bitcast.4, s32[1,512]{1,0:T(1,128)} %bitcast.5), custom_call_target="tpu_custom_call" | custom-call | flops 2000000000 | bytes 19000000 | tf_op jit(solution)/shard_map/graph_layer/pallas_call | solution.py:414
  72.6 0.0 copy-done.1
  72.6 0.0 copy-done
  72.7 1.2 %mix.1 = bf16[2048,256]{1,0:T(8,128)(2,1)} custom-call(bf16[2048,128]{1,0:T(8,128)(2,1)S(1)} %graph_layer.1.agg_ref, bf16[128,256]{1,0:T(8,128)(2,1)S(1)} %copy-done, f32[1,256]{1,0:T(1,128)S(1)} %bitcast.3), custom_call_target="tpu_custom_call" | custom-call | flops 200000000 | bytes 2000000 | tf_op jit(solution)/shard_map/mix/pallas_call | solution.py:426
Async XLA Ops:
  0.0 72.6 %copy-start.1 = (f32[256]{0:T(256)S(1)}, f32[256]{0:T(256)}, u32[]{:S(2)}) copy-start(f32[256]{0:T(256)} %param.11) | copy-start | bytes 3076
  0.0 72.6 %copy-start = (bf16[128,256]{1,0:T(8,128)(2,1)S(1)}, bf16[128,256]{1,0:T(8,128)(2,1)}, u32[]{:S(2)}) copy-start(bf16[128,256]{1,0:T(8,128)(2,1)} %w_ref.1) | copy-start | bytes 196612

commit v3 on v2

--- a/solution.py
+++ b/solution.py
@@ -10,25 +10,25 @@
 
 T = 128
 TILES = 512
+SAME = 384
 PAIRS = 320
 ROWS = 128
 OWN = 16
-CHUNKS = (32, 32, 32, 32)
-SENT_AS = (jnp.float32, jnp.float32, jnp.bfloat16, jnp.bfloat16)
-PAIRED_AS = (jnp.float32, jnp.float32, jnp.float32, jnp.bfloat16)
+CHUNKS = (48, 48, 32)
+SENT_AS = (jnp.float32, jnp.bfloat16, jnp.bfloat16)
+PAIRED_AS = (jnp.float32, jnp.float32, jnp.bfloat16)
 SCHEDULE = (
-    "0own", "1own", "2own", "load", "plan", "turn0", "turn1", "0hop", "0near", "turn2", "turn3", "turn4", "turn5",
-    "turn6", "turn7", "turn8", "turn9", "0far", "1hop", "turn10", "turn11", "turn12", "turn13", "turn14", "turn15",
-    "0near2", "0far2", "1wide", "2hop", "0end", "0b0", "1near2", "3own", "0b1", "0b2", "1far2", "0b3", "0b4", "0cut",
-    "2wide", "0y1", "3hop", "1end", "1b0", "2near2", "0y2", "1b1", "1b2", "2far2", "1b3", "1b4", "1cut", "3wide",
-    "0y3", "1y1", "2end", "2b0", "2b1", "2b2", "3near2", "3far2", "1y2", "2b3", "2b4", "2cut", "2y1", "3end", "3b0",
-    "2y2", "3cut", "1y3", "3y1", "2y3", "3y2", "3y3",
+    "0own", "1own", "2own", "load", "plan", "turn0", "turn1", "turn2", "turn3", "0hop", "0near", "turn4", "turn5",
+    "turn6", "turn7", "turn8", "turn9", "turn10", "turn11", "turn12", "turn13", "0far", "1hop", "turn14", "turn15",
+    "0near2", "0far2", "1wide", "2hop", "0end", "0b0", "0b1", "1near2", "0cut", "1far2", "0y1", "2wide", "0y2",
+    "1end", "1b0", "2near2", "1b1", "2far2", "1cut", "1y1", "0y3", "2end", "2b0", "1y2", "2cut", "2y1", "1y3", "2y2",
+    "2y3",
 )
 STAGE = 32
 STAGES = TILES // STAGE
 SLOTS = 4
-UNROLL = 32
-BLOCKS = 5
+UNROLL = 80
+BLOCKS = 2
 MSG = 20
 OUT_PARTS = 8
 F32 = jnp.float32
@@ -36,18 +36,22 @@
 I32 = jnp.int32
 
 
+def spot(i):
+    return (i & 1) * 2 + (i >> 1)
+
+
 def column(line):
     return jnp.broadcast_to(line, (T, T)).T
 
 
-def plan_tiles(trow_ref, tcol_ref, plan_v, last_v):
+def plan_tiles(trow_ref, tcol_ref, tile_v, block_v, same_v, last_v):
     row = trow_ref[...] & (ROWS - 1)
     tcol = tcol_ref[...]
-    at_z, at_x = (tcol >> 9) & 3, (tcol >> 7) & 3
-    col = ((at_z & 1) << 7) | ((at_z >> 1) << 6) | ((at_x & 1) << 5) | ((at_x >> 1) << 4) | (tcol & 15)
+    zi, xi = spot((tcol >> 9) & 3), spot((tcol >> 7) & 3)
+    block = jnp.where((tcol & 8) == 0, xi * 32 + zi * 8, 128 + zi * 32 + xi * 8) + (tcol & 7)
     k = lax.broadcasted_iota(I32, (1, TILES), 1)
     key = row * TILES + k
-    packed = k + (row << 10) + (col << 17) + 1
+    packed = k + (block << 10) + 1
     lane = lax.broadcasted_iota(I32, (T, T), 1)
     sub = lax.broadcasted_iota(I32, (T, T), 0)
     blocks = [slice(b * T, (b + 1) * T) for b in range(TILES // T)]
@@ -60,6 +64,10 @@
     odd = 2 * pairs - count
     through = jnp.sum(jnp.where(sub <= lane, column(pairs), 0), axis=0, keepdims=True)
     last_v[...] = jnp.where(count > 0, through - 1, -1)
+    first = column(jnp.where(count > 0, through - pairs, -1))
+    first = jnp.concatenate([first] * (SAME // T), axis=1)
+    starts = jnp.where(first == lax.broadcasted_iota(I32, (T, SAME), 1), 1, 0)
+    same_v[...] = 1 - jnp.sum(starts, axis=0, keepdims=True)
     total = jnp.zeros((1, 2 * PAIRS), I32)
     place = lax.broadcasted_iota(I32, (T, 2 * PAIRS), 1)
     for b in range(len(blocks)):
@@ -68,7 +76,8 @@
             at += jnp.sum(jnp.where(key[:, other] < key_s[b], 1, 0), axis=1, keepdims=True)
         packed_s = jnp.concatenate([column(packed[:, blocks[b]])] * (2 * PAIRS // T), axis=1)
         total += jnp.sum(jnp.where(place == at, packed_s, 0), axis=0, keepdims=True)
-    plan_v[...] = jnp.where(total == 0, TILES, total - 1)
+    tile_v[...] = jnp.where(total == 0, TILES, (total - 1) & 1023)
+    block_v[...] = jnp.where(total == 0, 0, (total - 1) >> 10)
 
 
 def kernel(feat_hbm, tiles_hbm, trow_hbm, tcol_hbm, out_ref, *scratch):
@@ -77,7 +86,9 @@
     take = lambda n: [scratch.pop(0) for _ in range(n)]
     xs = take(q_count)
     csend, crecv, own, ysend, yrecv = (take(q_count) for _ in range(5))
-    at, stage, slots, agg, plan_v, last_v, plan, last, feat_ref, trow_ref, tcol_ref = take(11)
+    at, stage, slots, agg, feat_ref, trow_ref, tcol_ref = take(7)
+    planned = take(4)
+    tile_of, block_of, same, last = lists = take(4)
     gsend, grecv, csem_s, csem_r, ysem_s, ysem_r, stage_sem, plan_sem, feat_sem = take(9)
 
     row, col = lax.axis_index("row"), lax.axis_index("col")
@@ -90,8 +101,8 @@
     def col_at(dy, c):
         return ((y + dy + 4) % 4) * 2 + c
 
-    def spot(i):
-        return (i % 2) * 2 + i // 2
+    def place(half, zi, xi):
+        return 128 + zi * 32 + xi * 8 if half else xi * 32 + zi * 8
 
     plane = {d: (row_at(*d), col) for d in ((1, 0), (-1, 0), (0, 1), (0, -1))}
     sibling = (row, y * 2 + 1 - core)
@@ -125,21 +136,20 @@
         block = feat_ref[t * T:(t + 1) * T, :].T
         start = 0
         for q, width in enumerate(CHUNKS):
-            xs[q][spot(z), spot(x), t] = block[start:start + width]
+            xs[q][place(t // 8, spot(z), spot(x)) + t % 8] = block[start:start + width]
             start += width
 
     pl.semaphore_wait(barrier, len(partners))
 
     def piece_of(q, piece, dz, dx):
-        kind, t0, n = piece
+        kind, half, t0, n = piece
         zi, xi = spot((z + dz + 4) % 4), spot((x + dx + 4) % 4)
         if kind == "shard":
-            return xs[q].at[zi, xi, pl.ds(t0, n)]
-        axis, near = kind
-        start = 2 * ((((z + dz + 4) if axis == 0 else (x + dx + 4)) + near) % 2)
-        if axis == 0:
-            return xs[q].at[pl.ds(start, 2), xi, pl.ds(t0, n)]
-        return xs[q].at[zi, pl.ds(start, 2), pl.ds(t0, n)]
+            start = place(half, zi, xi) + t0
+        else:
+            other = 2 * ((((x + dx) if half else (z + dz)) + 4 + kind) % 2)
+            start = place(half, zi, other) if half else place(half, other, xi)
+        return xs[q].at[pl.ds(start, n)]
 
     def message(q, m, direction, dz, dx, piece):
         part = piece_of(q, piece, dz, dx)
@@ -153,12 +163,12 @@
         for half in range(2):
             first = (lambda s: (s, 0)) if half == 0 else (lambda s: (0, s))
             second = (lambda s: (0, s)) if half == 0 else (lambda s: (s, 0))
-            t0, m0 = 8 * half, 10 * half
-            near, far = ((half, 1), t0, 8), ((half, 0), t0, 8)
-            table[m0 + 0] = (first(1), (0, 0), ("shard", t0, 8))
-            table[m0 + 1] = (first(-1), (0, 0), ("shard", t0, 8))
-            table[m0 + 2] = (first(1), first(-1), ("shard", t0, 4))
-            table[m0 + 3] = (first(-1), first(1), ("shard", t0 + 4, 4))
+            m0 = 10 * half
+            near, far = (1, half, 0, 16), (0, half, 0, 16)
+            table[m0 + 0] = (first(1), (0, 0), ("shard", half, 0, 8))
+            table[m0 + 1] = (first(-1), (0, 0), ("shard", half, 0, 8))
+            table[m0 + 2] = (first(1), first(-1), ("shard", half, 0, 4))
+            table[m0 + 3] = (first(-1), first(1), ("shard", half, 4, 4))
             table[m0 + 4] = (second(1), (0, 0), near)
             table[m0 + 5] = (second(-1), (0, 0), near)
             table[m0 + 6] = (second(1), (0, 0), far)
@@ -220,14 +230,13 @@
     def prepare():
         for copy in coordinates:
             copy.wait()
-        plan_tiles(trow_ref, tcol_ref, plan_v, last_v)
-        one = pltpu.make_async_copy(plan_v, plan, plan_sem.at[0])
-        two = pltpu.make_async_copy(last_v, last, plan_sem.at[1])
-        one.start()
-        two.start()
+        plan_tiles(trow_ref, tcol_ref, *planned)
+        copies = [pltpu.make_async_copy(planned[i], lists[i], plan_sem.at[i]) for i in range(4)]
+        for copy in copies:
+            copy.start()
         at[TILES] = jnp.zeros((T, T), BF16)
-        one.wait()
-        two.wait()
+        for copy in copies:
+            copy.wait()
 
     def products(q, p0, n, unroll=UNROLL):
         width = CHUNKS[q]
@@ -236,13 +245,10 @@
             def body(g, total):
                 for u in range(unroll):
                     p = p0 + g * unroll + u
-                    one, two = plan[0, 2 * p], plan[0, 2 * p + 1]
-                    before = plan[0, jnp.maximum(2 * p - 2, 0)]
-                    left = jnp.concatenate([pick(q, one), pick(q, two)], axis=1)
-                    right = jnp.concatenate([turned(one), turned(two)], axis=0)
+                    left = jnp.concatenate([pick(q, 2 * p), pick(q, 2 * p + 1)], axis=1)
+                    right = jnp.concatenate([turned(2 * p), turned(2 * p + 1)], axis=0)
                     product = lax.dot_general(left, right, NN, preferred_element_type=F32)
-                    same = ((one >> 10) & 127) == ((before >> 10) & 127)
-                    total = jnp.where(same, total, 0.0) + product
+                    total = jnp.where(same[0, p] == 1, total, 0.0) + product
                     slots[p, 0:width] = total
                 return total
 
@@ -250,11 +256,11 @@
             lax.fori_loop(0, n // unroll, body, first)
         return run
 
-    def pick(q, entry):
-        return xs[q][(entry >> 23) & 3, (entry >> 21) & 3, (entry >> 17) & 15]
-
-    def turned(entry):
-        return at[jnp.minimum(entry & 1023, TILES)]
+    def pick(q, p):
+        return xs[q][block_of[0, p] & 255]
+
+    def turned(p):
+        return at[jnp.minimum(tile_of[0, p], TILES)]
 
     ORDER = (2, -1, 1, 0)
 
@@ -347,7 +353,7 @@
         blocks = BLOCKS if q < q_count - 1 else 1
         step = PAIRS // blocks
         for b in range(blocks):
-            steps["%db%d" % (q, b)] = products(q, b * step, step, UNROLL if blocks > 1 else 2 * UNROLL)
+            steps["%db%d" % (q, b)] = products(q, b * step, step, UNROLL)
         for name, make in (("cut", extract), ("y1", reduce_first), ("y2", reduce_second), ("y3", reduce_last)):
             steps["%d%s" % (q, name)] = make(q)
 
@@ -383,7 +389,7 @@
     q_count = len(CHUNKS)
     widest = max(CHUNKS)
     dma = pltpu.SemaphoreType.DMA
-    scratch = [pltpu.VMEM((4, 4, OWN, f, T), BF16) for f in CHUNKS]
+    scratch = [pltpu.VMEM((16 * OWN, f, T), BF16) for f in CHUNKS]
     for kind in range(2):
         scratch += [pltpu.VMEM((4, OWN, f, T), kept) for f, kept in zip(CHUNKS, PAIRED_AS)]
     scratch += [pltpu.VMEM((4, OWN, f, T), F32) for f in CHUNKS]
@@ -394,13 +400,13 @@
         pltpu.VMEM((SLOTS, STAGE, T, T), BF16),
         pltpu.VMEM((PAIRS, widest, T), F32),
         pltpu.VMEM((OWN, T, T), BF16),
-        pltpu.VMEM((1, 2 * PAIRS), I32),
-        pltpu.VMEM((1, T), I32),
-        pltpu.SMEM((1, 2 * PAIRS), I32),
-        pltpu.SMEM((1, T), I32),
         pltpu.VMEM((OWN * T, T), BF16),
         pltpu.VMEM((1, TILES), I32),
         pltpu.VMEM((1, TILES), I32),
+    ]
+    lists = [(1, 2 * PAIRS), (1, 2 * PAIRS), (1, SAME), (1, T)]
+    scratch += [pltpu.VMEM(shape, I32) for shape in lists] + [pltpu.SMEM(shape, I32) for shape in lists]
+    scratch += [
         dma((q_count, MSG)),
         dma((q_count, MSG)),
         dma((q_count, 4)),
@@ -408,7 +414,7 @@
         dma((q_count, 6)),
         dma((q_count, 6)),
         dma((SLOTS,)),
-        dma((2,)),
+        dma((4,)),
         dma((4,)),
     ]
     aggregate = pl.pallas_call(

time: 74.2 us -> 68.4 us (0.922)
  Pallas kernels: 73.9 us -> 68.3 us
    pallas_call x1, Pallas kernels: 72.6 us -> 67 us  [local(): pl.pallas_call(kernel, out_shape=pltpu.VMEM((OWN * T, T), BF16), in_specs...]
where the time goes in v3:
time: 68.4 us; the launch traced here: 68.3 us
  Pallas kernels  68.3 us (100%)
    pallas_call x1, Pallas kernels, local(): pl.pallas_call(kernel, out_shape=pltpu.VMEM((OWN * T, T), BF16), in_specs...  67 us

profile of v3, /device:TPU:0, one launch (start us, length us, event | category | flops | bytes accessed | tf_op | source)
XLA Modules:
  0.0 68.3 jit_solution(7938437641265627679)
XLA Ops:
  0.0 0.0 copy-start.1
  0.0 0.0 copy-start
  0.0 67.0 %graph_layer.1.agg_ref = bf16[2048,128]{1,0:T(8,128)(2,1)S(1)} custom-call(bf16[2048,128]{1,0:T(8,128)(2,1)} %feat_hbm.1, bf16[512,128,128]{2,1,0:T(8,128)(2,1)} %tiles_hbm.1, s32[1,512]{1,0:T(1,128)} %bitcast.4, s32[1,512]{1,0:T(1,128)} %bitcast.5), custom_call_target="tpu_custom_call" | custom-call | flops 2000000000 | bytes 19000000 | tf_op jit(solution)/shard_map/graph_layer/pallas_call | solution.py:420
  67.0 0.0 copy-done.1
  67.1 0.0 copy-done
  67.1 1.2 %mix.1 = bf16[2048,256]{1,0:T(8,128)(2,1)} custom-call(bf16[2048,128]{1,0:T(8,128)(2,1)S(1)} %graph_layer.1.agg_ref, bf16[128,256]{1,0:T(8,128)(2,1)S(1)} %copy-done, f32[1,256]{1,0:T(1,128)S(1)} %bitcast.3), custom_call_target="tpu_custom_call" | custom-call | flops 200000000 | bytes 2000000 | tf_op jit(solution)/shard_map/mix/pallas_call | solution.py:432
Async XLA Ops:
  0.0 67.0 %copy-start.1 = (f32[256]{0:T(256)S(1)}, f32[256]{0:T(256)}, u32[]{:S(2)}) copy-start(f32[256]{0:T(256)} %param.11) | copy-start | bytes 3076
  0.0 67.0 %copy-start = (bf16[128,256]{1,0:T(8,128)(2,1)S(1)}, bf16[128,256]{1,0:T(8,128)(2,1)}, u32[]{:S(2)}) copy-start(bf16[128,256]{1,0:T(8,128)(2,1)} %w_ref.1) | copy-start | bytes 196612

commit v4 on v3

--- a/solution.py
+++ b/solution.py
@@ -277,54 +277,62 @@
             base = (((y + ORDER[o] + 4) % 4) * 2 + which) * OWN
 
             def body(g, carry):
-                for u in range(8):
-                    t = g * 8 + u
+                for u in range(OWN):
+                    t = g * OWN + u
                     p = last[0, base + t]
                     value = slots[jnp.clip(p, 0, PAIRS - 1), 0:width]
                     target[o, t] = jnp.where(p >= 0, value, 0.0).astype(target.dtype)
                 return carry
 
-            lax.fori_loop(0, OWN // 8, body, 0)
+            lax.fori_loop(0, 1, body, 0)
 
         def run():
             for o in range(4):
                 part(o, 1 - core, csend[q])
                 core_copy(q, o).start()
-            for o in range(4):
-                part(o, core, own[q])
+                if o > 0:
+                    part(o - 1, core, own[q])
+            part(3, core, own[q])
         return run
 
     Y_TARGET = (down, up, down, up, down, up)
 
-    def y_copy(q, n):
+    def cuts(q):
+        count = 2 if q == q_count - 1 else 1
+        return [(s, s * 8 // count, 8 // count) for s in range(count)]
+
+    def y_copy(q, n, s, first, rows):
+        part = pl.ds(first, rows)
         return pltpu.make_async_remote_copy(
-            src_ref=ysend[q].at[n], dst_ref=yrecv[q].at[n], send_sem=ysem_s.at[q, n], recv_sem=ysem_r.at[q, n],
-            device_id=Y_TARGET[n], device_id_type=MESH,
+            src_ref=ysend[q].at[n, part], dst_ref=yrecv[q].at[n, part], send_sem=ysem_s.at[q, 2 * n + s],
+            recv_sem=ysem_r.at[q, 2 * n + s], device_id=Y_TARGET[n], device_id_type=MESH,
         )
 
-    def joined(q, o, t0):
-        return own[q][o, t0:t0 + 8] + crecv[q][o, t0:t0 + 8].astype(F32)
+    def joined(q, o, t0, rows):
+        return own[q][o, t0:t0 + rows] + crecv[q][o, t0:t0 + rows].astype(F32)
 
     def reduce_first(q):
         def run():
             core_copy(q, 0).wait_recv()
-            for n in range(2):
-                ysend[q][n] = joined(q, 0, 8 * n).astype(SENT_AS[q])
-                y_copy(q, n).start()
-            core_copy(q, 1).wait_recv()
-            ysend[q][2] = joined(q, 1, 8).astype(SENT_AS[q])
-            y_copy(q, 2).start()
-            core_copy(q, 2).wait_recv()
-            ysend[q][3] = joined(q, 2, 0).astype(SENT_AS[q])
-            y_copy(q, 3).start()
+            for s, first, rows in cuts(q):
+                for n in range(2):
+                    ysend[q][n, first:first + rows] = joined(q, 0, 8 * n + first, rows).astype(SENT_AS[q])
+                    y_copy(q, n, s, first, rows).start()
+            for n, o, t0 in ((2, 1, 8), (3, 2, 0)):
+                core_copy(q, o).wait_recv()
+                for s, first, rows in cuts(q):
+                    ysend[q][n, first:first + rows] = joined(q, o, t0 + first, rows).astype(SENT_AS[q])
+                    y_copy(q, n, s, first, rows).start()
         return run
 
     def reduce_second(q):
         def run():
-            for n, o, t0 in ((4, 1, 0), (5, 2, 8)):
-                y_copy(q, n - 4).wait_recv()
-                ysend[q][n] = (joined(q, o, t0) + yrecv[q][n - 4].astype(F32)).astype(SENT_AS[q])
-                y_copy(q, n).start()
+            for s, first, rows in cuts(q):
+                for n, o, t0 in ((4, 1, 0), (5, 2, 8)):
+                    y_copy(q, n - 4, s, first, rows).wait_recv()
+                    value = joined(q, o, t0 + first, rows) + yrecv[q][n - 4, first:first + rows].astype(F32)
+                    ysend[q][n, first:first + rows] = value.astype(SENT_AS[q])
+                    y_copy(q, n, s, first, rows).start()
         return run
 
     def reduce_last(q):
@@ -332,12 +340,13 @@
 
         def run():
             core_copy(q, 3).wait_recv()
-            for half, direct, summed in ((0, 3, 4), (1, 2, 5)):
-                y_copy(q, direct).wait_recv()
-                y_copy(q, summed).wait_recv()
-                t0 = 8 * half
-                value = joined(q, 3, t0) + yrecv[q][direct].astype(F32) + yrecv[q][summed].astype(F32)
-                agg[t0:t0 + 8, start:start + CHUNKS[q]] = value.astype(BF16)
+            for s, first, rows in cuts(q):
+                for half, direct, summed in ((0, 3, 4), (1, 2, 5)):
+                    y_copy(q, direct, s, first, rows).wait_recv()
+                    y_copy(q, summed, s, first, rows).wait_recv()
+                    t0, part = 8 * half + first, slice(first, first + rows)
+                    value = joined(q, 3, t0, rows) + yrecv[q][direct, part].astype(F32) + yrecv[q][summed, part].astype(F32)
+                    agg[t0:t0 + rows, start:start + CHUNKS[q]] = value.astype(BF16)
         return run
 
     def begin():
@@ -353,7 +362,7 @@
         blocks = BLOCKS if q < q_count - 1 else 1
         step = PAIRS // blocks
         for b in range(blocks):
-            steps["%db%d" % (q, b)] = products(q, b * step, step, UNROLL)
+            steps["%db%d" % (q, b)] = products(q, b * step, step, UNROLL if q < q_count - 1 else 2 * UNROLL)
         for name, make in (("cut", extract), ("y1", reduce_first), ("y2", reduce_second), ("y3", reduce_last)):
             steps["%d%s" % (q, name)] = make(q)
 
@@ -368,7 +377,8 @@
         for o in range(4):
             core_copy(q, o).wait_send()
         for n in range(6):
-            y_copy(q, n).wait_send()
+            for s, first, rows in cuts(q):
+                y_copy(q, n, s, first, rows).wait_send()
 
 
 def mix(agg_ref, w_ref, bias_ref, out_hbm, out_v, sem):
@@ -411,8 +421,8 @@
         dma((q_count, MSG)),
         dma((q_count, 4)),
         dma((q_count, 4)),
-        dma((q_count, 6)),
-        dma((q_count, 6)),
+        dma((q_count, 12)),
+        dma((q_count, 12)),
         dma((SLOTS,)),
         dma((4,)),
         dma((4,)),

time: 68.4 us -> 68.1 us (level)
  no operation moved by 1% of the time
where the time goes in v4:
time: 68.1 us; the launch traced here: 68 us
  Pallas kernels  68 us (100%)
    pallas_call x1, Pallas kernels, local(): pl.pallas_call(kernel, out_shape=pltpu.VMEM((OWN * T, T), BF16), in_specs...  66.7 us

profile of v4, /device:TPU:0, one launch (start us, length us, event | category | flops | bytes accessed | tf_op | source)
XLA Modules:
  0.0 68.0 jit_solution(15269812804036891463)
XLA Ops:
  0.0 0.0 copy-start.1
  0.0 0.0 copy-start
  0.0 66.7 %graph_layer.1.agg_ref = bf16[2048,128]{1,0:T(8,128)(2,1)S(1)} custom-call(bf16[2048,128]{1,0:T(8,128)(2,1)} %feat_hbm.1, bf16[512,128,128]{2,1,0:T(8,128)(2,1)} %tiles_hbm.1, s32[1,512]{1,0:T(1,128)} %bitcast.4, s32[1,512]{1,0:T(1,128)} %bitcast.5), custom_call_target="tpu_custom_call" | custom-call | flops 2000000000 | bytes 19000000 | tf_op jit(solution)/shard_map/graph_layer/pallas_call | solution.py:430
  66.8 0.0 copy-done.1
  66.8 0.0 copy-done
  66.8 1.2 %mix.1 = bf16[2048,256]{1,0:T(8,128)(2,1)} custom-call(bf16[2048,128]{1,0:T(8,128)(2,1)S(1)} %graph_layer.1.agg_ref, bf16[128,256]{1,0:T(8,128)(2,1)S(1)} %copy-done, f32[1,256]{1,0:T(1,128)S(1)} %bitcast.3), custom_call_target="tpu_custom_call" | custom-call | flops 200000000 | bytes 2000000 | tf_op jit(solution)/shard_map/mix/pallas_call | solution.py:442
Async XLA Ops:
  0.0 66.8 %copy-start.1 = (f32[256]{0:T(256)S(1)}, f32[256]{0:T(256)}, u32[]{:S(2)}) copy-start(f32[256]{0:T(256)} %param.11) | copy-start | bytes 3076
  0.0 66.8 %copy-start = (bf16[128,256]{1,0:T(8,128)(2,1)S(1)}, bf16[128,256]{1,0:T(8,128)(2,1)}, u32[]{:S(2)}) copy-start(bf16[128,256]{1,0:T(8,128)(2,1)} %w_ref.1) | copy-start | bytes 196612
